TPU v7x, 32 devices: a whole 2x2x4 slice. The times are simulated.
32 devices in a mesh: dp: 8 (over z, core), fsdp: 4 (over y, x).
Axes of the slice: x: 2, y: 2, z: 4, core: 2. Of those that a mesh axis runs over, the one named last changes fastest.
Arguments:
- patches: bfloat16 [8192, 384], P(('dp', 'fsdp')), may hold values from -6 to 6
- grad_embed: bfloat16 [8192, 3072], P(('dp', 'fsdp')), may hold values from -6 to 6
- weight: bfloat16 [384, 3072], P(None, 'fsdp'), may hold values from -0.3125 to 0.3125
- straggler: int32 [8], P('dp'), may hold values 0 or 1
- decode: int32 [8], P('dp'), may hold values from 1 to 3
- encode: int32 [8, 2], P('dp'), may hold values from 1 to 3
Outputs:
- embedded: bfloat16 [8192, 3072], P(('dp', 'fsdp'))
- weight_grad: float32 [384, 3072], P('dp', 'fsdp')
All inputs are finite; a program needn't handle non-finite values. No bound on the sum of `straggler` on one device may be relied on, other than what follows from the above.
Results may differ from a plain program's by a relative error of at most 0.001.
Values may be sent and summed in bfloat16 or wider, within the bound.
No kernel may reach another device: no remote copies, remote signals or barrier semaphores. Data moves between devices by JAX's collectives and lax.ppermute only.
A program may use at most 64 MiB of HBM per device.

v0:
```python
import functools
import math

import jax
import jax.numpy as jnp
from jax import lax
from jax.experimental import pallas as pl
from jax.experimental.pallas import tpu as pltpu
from jax.sharding import PartitionSpec as P

LANES = 128
TAIL = 16
STEP = math.log(2) / 16
TOP = 32760.0
F32, BF16, I16, I32 = jnp.float32, jnp.bfloat16, jnp.int16, jnp.int32
VMEM = pl.BlockSpec(memory_space=pltpu.VMEM)
SMEM = pl.BlockSpec(memory_space=pltpu.SMEM)
HBM = pl.BlockSpec(memory_space=pltpu.HBM)


def in_hbm(array):
    return pltpu.with_memory_space_constraint(array, pltpu.HBM)


def exchange(block, axis, step):
    return lax.ppermute(block, axis, [(i, i ^ step) for i in range(lax.axis_size(axis))])


def shifted(block, axis, distance):
    count = lax.axis_size(axis)
    return lax.ppermute(block, axis, [((i - distance) % count, i) for i in range(count)])


def times(a, b, dims=((1,), (0,))):
    return lax.dot_general(a, b, (dims, ((), ())), preferred_element_type=F32)


def chunk_shape(rows, columns):
    return (columns // LANES * rows + TAIL, LANES)


def put_chunk(ref, blocks, extra=()):
    rows = blocks[0].shape[0]
    tail = jnp.zeros((TAIL, LANES), I32)
    row = lax.broadcasted_iota(I32, (TAIL, LANES), 0)
    for j, block in enumerate(blocks):
        largest = jnp.max(jnp.abs(block), axis=0, keepdims=True)
        power = jnp.ceil(jnp.log(jnp.maximum(largest, 2.0**-100)) * (1 / STEP))
        coded = block * (TOP * jnp.exp(power * -STEP))
        ref[pl.ds(j * rows, rows), :] = coded.astype(I32).astype(I16)
        tail = jnp.where(row == j, power.astype(I32), tail)
    for j, number in enumerate(extra):
        tail = jnp.where(row == TAIL - len(extra) + j, number, tail)
    ref[pl.ds(len(blocks) * rows, TAIL), :] = tail.astype(I16)


def get_chunk(ref, rows):
    count = (ref.shape[0] - TAIL) // rows
    tail = ref[pl.ds(count * rows, TAIL), :].astype(F32)
    scale = jnp.exp(tail * STEP) * (1 / TOP)
    return [ref[pl.ds(j * rows, rows), :].astype(F32) * scale[j : j + 1, :] for j in range(count)], tail


def lanes(j):
    return slice(j * LANES, (j + 1) * LANES)


def send_kernel(depth, place, patches, grad_embed, shares, sent, left, held, p_held, arrived):
    me, core = place[0], place[2]
    count, _, columns = held.shape
    blocks, features = columns // LANES, patches.shape[1]
    rows = features // 2
    copies = [pltpu.make_async_copy(patches, p_held, arrived.at[count])]
    for k in range(count):
        here = pl.ds(pl.multiple_of((me ^ k) * columns, columns), columns)
        copies.append(pltpu.make_async_copy(grad_embed.at[:, here], held.at[k], arrived.at[k]))
    for copy in copies:
        copy.start()
    extra = shares[:, 0:1], shares[:, 1:2]
    i = lax.broadcasted_iota(I32, (features, features), 0)
    j = lax.broadcasted_iota(I32, (features, features), 1)
    half, i = i // rows, i % rows
    chosen = jnp.where(j == (i // depth * 2 + (core ^ half)) * depth + i % depth, 1.0, 0.0).astype(BF16)
    copies[0].wait()
    turned = times(chosen, p_held[...], ((1,), (1,))).astype(BF16)
    left[...] = turned[:rows]
    for k in range(count):
        copies[1 + k].wait()
        value = times(turned[rows:], held[k])
        put_chunk(sent.at[k], [value[:, lanes(j)] for j in range(blocks)], extra)


def own_kernel(left, held, kept):
    for k in range(kept.shape[0]):
        value = times(left[...], held[k])
        for j in range(kept.shape[1]):
            kept[k, j] = value[:, lanes(j)]


def pair_kernel(bounds, place, tokens, kept, came, shares, before, before_sib, *outs):
    core = place[2]
    rows = kept.shape[2]
    first, second = shares[:, 0:1].astype(F32), shares[:, 1:2].astype(F32)
    tail = get_chunk(came.at[0], rows)[1]
    first_sib, second_sib = (tail[TAIL - 2 + j : TAIL - 1 + j, 0:1] for j in range(2))
    even = core == 0
    carried = jnp.where(even, before[:, 1:2], before_sib[:, 1:2]).astype(F32)
    scale = (first + jnp.where(even, carried, second_sib)) / tokens[0].astype(F32)
    scale_sib = (first_sib + jnp.where(even, second, carried)) / tokens[0].astype(F32)
    for (lo, hi), still, sent in zip(bounds, outs[::2], outs[1::2]):

        def value(k):
            parts, _ = get_chunk(came.at[k], rows)
            return [scale * kept[k, j] + scale_sib * parts[j] for j in range(lo, hi)]

        put_chunk(sent.at[0], value(1 + core))
        put_chunk(sent.at[1], value(3))
        for at, k in enumerate((0, 2 - core)):
            for j, part in enumerate(value(k)):
                still[at, j] = part


def step_kernel(kept, came, still, sent):
    _, blocks, rows, _ = kept.shape
    parts, _ = get_chunk(came.at[1], rows)
    put_chunk(sent, [kept[1, j] + part for j, part in enumerate(parts)])
    for j, part in enumerate(get_chunk(came.at[0], rows)[0]):
        still[j] = kept[0, j] + part


def middle_kernel(depth, place, kept, came, *refs):
    *outs, held = refs
    blocks, rows, _ = kept.shape
    for j, part in enumerate(get_chunk(came, rows)[0]):
        held[j] = kept[j] + part
    for k, out in enumerate(outs):
        here = pl.ds(pl.multiple_of((place[1] ^ k) * depth, depth), depth)
        put_chunk(out, [held[j, here, :] for j in range(blocks)])


def last_kernel(bounds, *refs):
    *ins, out = refs
    count = len(ins) // len(bounds)
    for i, (lo, _) in enumerate(bounds):
        parts = [get_chunk(ref, out.shape[0])[0] for ref in ins[i * count : (i + 1) * count]]
        for j, terms in enumerate(zip(*parts)):
            out[:, lanes(lo + j)] = sum(terms[1:], terms[0])


def half_kernel(place, first, half):
    rows = half.shape[0]
    half[...] = first[pl.ds(pl.multiple_of(place[2] * rows, rows), rows), :]


def near_kernel(place, patches, own, first, second, out, p_held, held, arrived):
    core = place[2]
    copies = [
        pltpu.make_async_copy(patches, p_held, arrived.at[0]),
        pltpu.make_async_copy(own, held, arrived.at[1]),
    ]
    for copy in copies:
        copy.start()
    copies[0].wait()
    out[1 + core] = times(p_held[...], first[...]).astype(BF16)
    out[2 - core] = times(p_held[...], second[...]).astype(BF16)
    copies[1].wait()
    out[0] = times(p_held[...], held[...]).astype(BF16)


def embed_kernel(place, patches, near, far, far_sib, out, p_held, halves, arrived):
    me, core, columns = place[0], place[2], near.shape[2]
    rows = far.shape[0]
    copy = pltpu.make_async_copy(patches, p_held, arrived)
    copy.start()

    def put(k, value):
        out[:, pl.ds(pl.multiple_of((me ^ k) * columns, columns), columns)] = value

    for k in range(3):
        put(k, near[k])
    copy.wait()
    halves[0] = p_held[:, :rows]
    halves[1] = p_held[:, rows:]
    put(3, (times(halves[core], far[...]) + times(halves[1 - core], far_sib[...])).astype(BF16))


def call(kernel, outs, operands, specs=(), scratch=(), flops=0):
    moved = sum(math.prod(a.shape) * a.dtype.itemsize for a in [*operands, *jax.tree.leaves(outs)]) if flops else 0
    return pl.pallas_call(
        kernel,
        out_shape=outs,
        in_specs=[*specs] + [VMEM] * (len(operands) - len(specs)),
        out_specs=jax.tree.map(lambda _: VMEM, outs),
        scratch_shapes=scratch,
        compiler_params=pltpu.CompilerParams(vmem_limit_bytes=24 * 2**20),
        cost_estimate=pl.CostEstimate(flops=flops, bytes_accessed=moved, transcendentals=0),
    )(*operands)


def tiled_body(patches, grad_embed, weight, straggler, decode, encode):
    count_dp, count_fsdp = lax.axis_size("dp"), lax.axis_size("fsdp")
    dp, me = lax.axis_index("dp"), lax.axis_index("fsdp")
    core = dp % 2
    place = jnp.stack([me, dp // 2, core])
    tokens, features = patches.shape
    columns = weight.shape[1]
    rows, depth, blocks = features // 2, features // count_dp, columns // LANES
    chunk = chunk_shape(rows, columns)
    bounds = [(0, blocks // 2), (blocks // 2, blocks)]

    def along_planes(block, step, replicas):
        pairs = [(d * 4 + f, d * 4 + (f ^ step(d % 2))) for d in replicas for f in range(4)]
        return lax.ppermute(block, ("dp", "fsdp"), pairs)

    with jax.named_scope("gather_weight"):
        first = along_planes(weight, lambda c: 1 + c, range(count_dp))

    with jax.named_scope("shares"):
        shares = encode * straggler[:, None] * decode[:, None]
        before = shifted(shares, "dp", 1)
    with jax.named_scope("send"):
        sent, left, held = call(
            functools.partial(send_kernel, depth),
            [
                jax.ShapeDtypeStruct((count_fsdp, *chunk), I16),
                jax.ShapeDtypeStruct((rows, tokens), BF16),
                jax.ShapeDtypeStruct((count_fsdp, tokens, columns), BF16),
            ],
            [place, in_hbm(patches), in_hbm(grad_embed), shares],
            [SMEM, HBM, HBM],
            [pltpu.VMEM(patches.shape, BF16), pltpu.SemaphoreType.DMA((count_fsdp + 1,))],
        )
    with jax.named_scope("own"):
        kept = call(
            own_kernel,
            jax.ShapeDtypeStruct((count_fsdp, blocks, rows, LANES), F32),
            [left, held],
            flops=10**11,
        )
        first, kept = lax.optimization_barrier((first, kept))
    with jax.named_scope("relay_weight"):
        second = exchange(first, "dp", 1)
        half = call(
            half_kernel,
            jax.ShapeDtypeStruct((rows, columns), BF16),
            [place, first],
            [SMEM],
        )
        far = along_planes(half, lambda c: 2 - c, range(count_dp))
    with jax.named_scope("pair"):
        came = exchange(sent, "dp", 1)
        before_sib = exchange(before, "dp", 1)
        outs = call(
            functools.partial(pair_kernel, bounds),
            [
                shape
                for lo, hi in bounds
                for shape in (
                    jax.ShapeDtypeStruct((2, hi - lo, rows, LANES), F32),
                    jax.ShapeDtypeStruct((2, *chunk_shape(rows, (hi - lo) * LANES)), I16),
                )
            ],
            [place, jnp.full((1,), tokens * count_fsdp, I32), kept, came, shares, before, before_sib],
            [SMEM] * 2,
            flops=10**11,
        )
        kept_parts = list(outs[::2])
        came_parts = [along_planes(sent, lambda c: 1 + c, range(count_dp)) for sent in outs[1::2]]
    with jax.named_scope("embed_near"):
        far, second = lax.optimization_barrier((far, second))
        near = call(
            near_kernel,
            jax.ShapeDtypeStruct((3, tokens, columns), BF16),
            [place, in_hbm(patches), in_hbm(weight), first, second],
            [SMEM, HBM, HBM],
            [pltpu.VMEM(patches.shape, BF16), pltpu.VMEM(weight.shape, BF16), pltpu.SemaphoreType.DMA((2,))],
            flops=2 * 10**9,
        )
        near, came_parts[0] = lax.optimization_barrier((near, came_parts[0]))
    with jax.named_scope("steps"):
        for i, (lo, hi) in enumerate(bounds):
            kept_parts[i], sent = call(
                step_kernel,
                [
                    jax.ShapeDtypeStruct((hi - lo, rows, LANES), F32),
                    jax.ShapeDtypeStruct(chunk_shape(rows, (hi - lo) * LANES), I16),
                ],
                [kept_parts[i], came_parts[i]],
                flops=(0, 10**10)[i],
            )
            came_parts[i] = along_planes(sent, lambda c: 2 - c, range(count_dp))
    with jax.named_scope("relay_weight"):
        far, kept_parts[1] = lax.optimization_barrier((far, kept_parts[1]))
        far_sib = exchange(far, "dp", 1)
    with jax.named_scope("middle"):
        sums = []
        for i, (lo, hi) in enumerate(bounds):
            if i and 1:
                came_parts[i], sums[1] = lax.optimization_barrier((came_parts[i], sums[1]))
            parts = call(
                functools.partial(middle_kernel, depth),
                [jax.ShapeDtypeStruct(chunk_shape(depth, (hi - lo) * LANES), I16)] * (count_dp // 2),
                [place, kept_parts[i], came_parts[i]],
                [SMEM],
                [pltpu.VMEM((hi - lo, rows, LANES), F32)],
                flops=10**10,
            )
            sums += [exchange(part, "dp", 2 * k) if k else part for k, part in enumerate(parts)]
    with jax.named_scope("embed"):
        near, sums[count_dp // 2] = lax.optimization_barrier((near, sums[count_dp // 2]))
        embedded = call(
            embed_kernel,
            jax.ShapeDtypeStruct((tokens, columns * count_fsdp), BF16),
            [place, in_hbm(patches), near, far, far_sib],
            [SMEM, HBM],
            [pltpu.VMEM(patches.shape, BF16), pltpu.VMEM((2, tokens, rows), BF16), pltpu.SemaphoreType.DMA],
            flops=10**10,
        )
    with jax.named_scope("last"):
        embedded, *sums = lax.optimization_barrier((embedded, *sums))
        decoded = call(
            functools.partial(last_kernel, bounds), jax.ShapeDtypeStruct((depth, columns), F32), sums
        )
    return embedded, decoded


def plain_body(patches, grad_embed, weight, straggler, decode, encode):
    shares = (straggler * decode)[:, None] * encode
    factor = (shares[:, 0] + shifted(shares[:, 1], "dp", 1))[0]
    scale = factor.astype(F32) / (patches.shape[0] * lax.axis_size("fsdp"))
    whole = lax.all_gather(weight, "fsdp", axis=1, tiled=True)
    embedded = times(patches, whole).astype(BF16)
    term = scale * times(grad_embed, patches, ((0,), (0,)))
    term = lax.psum_scatter(term, "fsdp", scatter_dimension=0, tiled=True)
    return embedded, lax.psum_scatter(term.T, "dp", scatter_dimension=0, tiled=True)


def body(patches, grad_embed, weight, straggler, decode, encode):
    fits = patches.shape[1] % (16 * lax.axis_size("dp")) == 0 and weight.shape[1] % LANES == 0
    fits = fits and lax.axis_size("fsdp") == 4
    run = tiled_body if fits else plain_body
    return run(patches, grad_embed, weight, straggler, decode, encode)


def solution(mesh):
    return jax.shard_map(
        body,
        mesh=mesh,
        in_specs=(
            P(("dp", "fsdp"), None),
            P(("dp", "fsdp"), None),
            P(None, "fsdp"),
            P("dp"),
            P("dp"),
            P("dp", None),
        ),
        out_specs=(P(("dp", "fsdp"), None), P("dp", "fsdp")),
        check_vma=False,
    )
```

profile of v0, /device:TPU:0, one launch (start us, length us, event | category | flops | bytes accessed | tf_op | source)
XLA Modules:
  0.0 45.2 jit_solution(17132285441042382047)
XLA Ops:
  0.6 3.0 %collective-permute-start = (bf16[384,768]{1,0:T(8,128)(2,1)}, bf16[384,768]{1,0:T(8,128)(2,1)S(1)}, u32[]{:S(2)}, u32[]{:S(2)}) collective-permute-start(bf16[384,768]{1,0:T(8,128)(2,1)} %own.3), channel_id=1, source_target_pairs={{0,1},{1,0},{2,3},{3,2},{4,6},{5,7},{6,4},{7,5},{8,9},{9,8},{10,11... | collective-permute-start | bytes 1769480 | tf_op jit(solution)/shard_map/gather_weight/ppermute | solution.py:213
  4.9 0.7 %multiply_multiply_fusion.shares = s32[1,2]{1,0:T(1,128)S(1)} fusion(s32[1,2]{1,0:T(1,128)} %param.11, s32[]{:T(128)} %bitcast.6, s32[]{:T(128)} %bitcast.5), kind=kLoop, calls=%fused_computation.1 | loop fusion | flops 4 | bytes 24 | tf_op jit(solution)/shard_map/shares/mul | solution.py:219
  5.7 3.4 %send.1 = (s16[4,1168,128]{2,1,0:T(8,128)(2,1)S(1)}, bf16[192,256]{1,0:T(8,128)(2,1)S(1)}, bf16[4,256,768]{2,1,0:T(8,128)(2,1)S(1)}) custom-call(s32[3]{0:T(128)S(1)} %pad_add_fusion.place, bf16[256,384]{1,0:T(8,128)(2,1)} %patches.5, bf16[256,3072]{1,0:T(8,128)(2,1)} %grad_embed.1, s32[1,2]{1,0:T(1,128)S(1)} %multiply_multiply_fusion.shares), custom_call_target="tpu_custom_call" | custom-call | tf_op jit(solution)/shard_map/send/pallas_call | solution.py:189
  9.0 1.8 %collective-permute-start.3 = (s16[4,1168,128]{2,1,0:T(8,128)(2,1)S(1)}, s16[4,1168,128]{2,1,0:T(8,128)(2,1)S(1)}, u32[]{:S(2)}, u32[]{:S(2)}) collective-permute-start(s16[4,1168,128]{2,1,0:T(8,128)(2,1)S(1)} %get-tuple-element.47), channel_id=1, source_target_pairs={{0,4},{4,0},{8,12},{12,8},{16,20},{20,16},{24,28},{28,24},{1,5},{5... | collective-permute-start | bytes 3588104 | tf_op jit(solution)/shard_map/pair/ppermute | solution.py:26
  11.7 0.6 %relay_weight.1 = bf16[192,768]{1,0:T(8,128)(2,1)S(1)} custom-call(s32[3]{0:T(128)S(1)} %pad_add_fusion.place, bf16[384,768]{1,0:T(8,128)(2,1)S(1)} %collective-permute-done.first), custom_call_target="tpu_custom_call" | custom-call | tf_op jit(solution)/shard_map/relay_weight/pallas_call | solution.py:189
  12.5 2.0 %collective-permute-start.1 = (bf16[192,768]{1,0:T(8,128)(2,1)S(1)}, bf16[192,768]{1,0:T(8,128)(2,1)S(1)}, u32[]{:S(2)}, u32[]{:S(2)}) collective-permute-start(bf16[192,768]{1,0:T(8,128)(2,1)S(1)} %relay_weight.1), channel_id=1, source_target_pairs={{0,2},{1,3},{2,0},{3,1},{4,5},{5,4},{6,7},{7,6},{8,10},{9,11},{10,... | collective-permute-start | bytes 884744 | tf_op jit(solution)/shard_map/relay_weight/ppermute | solution.py:213
  14.5 1.4 %pair.1 = (f32[2,3,192,128]{3,2,1,0:T(8,128)S(1)}, s16[2,592,128]{2,1,0:T(8,128)(2,1)S(1)}, f32[2,3,192,128]{3,2,1,0:T(8,128)S(1)}, s16[2,592,128]{2,1,0:T(8,128)(2,1)S(1)}) custom-call(s32[3]{0:T(128)S(1)} %pad_add_fusion.place, s32[1]{0:T(128)} %constant.34.clone.1.tokens, f32[4,6,192,128]{3,2,1,0:T(8,128)S(1)} %own.2.kept, ...), custom_call_target="tpu_custom_call" | custom-call | flops 99999997952 | bytes 5341224 | tf_op jit(solution)/shard_map/pair/pallas_call | solution.py:189
  15.9 1.6 %collective-permute-start.6 = (s16[2,592,128]{2,1,0:T(8,128)(2,1)S(1)}, s16[2,592,128]{2,1,0:T(8,128)(2,1)S(1)}, u32[]{:S(2)}, u32[]{:S(2)}) collective-permute-start(s16[2,592,128]{2,1,0:T(8,128)(2,1)S(1)} %get-tuple-element.48), channel_id=1, source_target_pairs={{0,1},{1,0},{2,3},{3,2},{4,6},{5,7},{6,4},{7,5},{8,9},{9,8},{10,11... | collective-permute-start | bytes 909320 | tf_op jit(solution)/shard_map/pair/ppermute | solution.py:213
  17.4 0.5 %collective-permute-start.7 = (s16[2,592,128]{2,1,0:T(8,128)(2,1)S(1)}, s16[2,592,128]{2,1,0:T(8,128)(2,1)S(1)}, u32[]{:S(2)}, u32[]{:S(2)}) collective-permute-start(s16[2,592,128]{2,1,0:T(8,128)(2,1)S(1)} %get-tuple-element.52), channel_id=1, source_target_pairs={{0,1},{1,0},{2,3},{3,2},{4,6},{5,7},{6,4},{7,5},{8,9},{9,8},{10,11... | collective-permute-start | bytes 909320 | tf_op jit(solution)/shard_map/pair/ppermute | solution.py:213
  18.0 1.7 %collective-permute-done.1.far = bf16[192,768]{1,0:T(8,128)(2,1)S(1)} collective-permute-done((bf16[192,768]{1,0:T(8,128)(2,1)S(1)}, bf16[192,768]{1,0:T(8,128)(2,1)S(1)}, u32[]{:S(2)}, u32[]{:S(2)}) %collective-permute-start.1) | collective-permute-done | bytes 294944 | tf_op jit(solution)/shard_map/relay_weight/ppermute | solution.py:213
  19.7 2.6 %embed_near.1.near = bf16[3,256,768]{2,1,0:T(8,128)(2,1)S(1)} custom-call(s32[3]{0:T(128)S(1)} %pad_add_fusion.place, bf16[256,384]{1,0:T(8,128)(2,1)} %patches.5, bf16[384,768]{1,0:T(8,128)(2,1)} %own.3, bf16[384,768]{1,0:T(8,128)(2,1)S(1)} %collective-permute-done.first, bf16[384,768]{1,0:T(8,128)(2,1)S(1)} %collective-permute-done.2.second), custom_call_target="tpu_custom_call" | custom-call | flops 2000000000 | bytes 3145740 | tf_op jit(solution)/shard_map/embed_near/pallas_call | solution.py:189
  22.9 2.0 %collective-permute-start.9 = (s16[592,128]{1,0:T(8,128)(2,1)S(1)}, s16[592,128]{1,0:T(8,128)(2,1)S(1)}, u32[]{:S(2)}, u32[]{:S(2)}) collective-permute-start(s16[592,128]{1,0:T(8,128)(2,1)S(1)} %get-tuple-element.59), channel_id=1, source_target_pairs={{0,2},{1,3},{2,0},{3,1},{4,5},{5,4},{6,7},{7,6},{8,10},{9,11},{10,... | collective-permute-start | bytes 454664 | tf_op jit(solution)/shard_map/steps/ppermute | solution.py:213
  24.9 1.4 %collective-permute-done.7.came = s16[2,592,128]{2,1,0:T(8,128)(2,1)S(1)} collective-permute-done((s16[2,592,128]{2,1,0:T(8,128)(2,1)S(1)}, s16[2,592,128]{2,1,0:T(8,128)(2,1)S(1)}, u32[]{:S(2)}, u32[]{:S(2)}) %collective-permute-start.7) | collective-permute-done | bytes 303136 | tf_op jit(solution)/shard_map/pair/ppermute | solution.py:213
  26.5 0.9 %collective-permute-start.8 = (s16[592,128]{1,0:T(8,128)(2,1)S(1)}, s16[592,128]{1,0:T(8,128)(2,1)S(1)}, u32[]{:S(2)}, u32[]{:S(2)}) collective-permute-start(s16[592,128]{1,0:T(8,128)(2,1)S(1)} %get-tuple-element.55), channel_id=1, source_target_pairs={{0,2},{1,3},{2,0},{3,1},{4,5},{5,4},{6,7},{7,6},{8,10},{9,11},{10,... | collective-permute-start | bytes 454664 | tf_op jit(solution)/shard_map/steps/ppermute | solution.py:213
  27.4 0.8 %collective-permute-done.9.came = s16[592,128]{1,0:T(8,128)(2,1)S(1)} collective-permute-done((s16[592,128]{1,0:T(8,128)(2,1)S(1)}, s16[592,128]{1,0:T(8,128)(2,1)S(1)}, u32[]{:S(2)}, u32[]{:S(2)}) %collective-permute-start.9) | collective-permute-done | bytes 151584 | tf_op jit(solution)/shard_map/steps/ppermute | solution.py:213
  28.2 0.7 %middle.2 = (s16[160,128]{1,0:T(8,128)(2,1)S(1)}, s16[160,128]{1,0:T(8,128)(2,1)S(1)}, s16[160,128]{1,0:T(8,128)(2,1)S(1)}, s16[160,128]{1,0:T(8,128)(2,1)S(1)}) custom-call(s32[3]{0:T(128)S(1)} %pad_add_fusion.place, f32[3,192,128]{2,1,0:T(8,128)S(1)} %get-tuple-element.58.kept, s16[592,128]{1,0:T(8,128)(2,1)S(1)} %collective-permute-done.9.came), custom_call_target="tpu_custom_call" | custom-call | flops 10000000000 | bytes 610316 | tf_op jit(solution)/shard_map/middle/pallas_call | solution.py:189
  28.9 2.1 %collective-permute-start.10 = (s16[160,128]{1,0:T(8,128)(2,1)S(1)}, s16[160,128]{1,0:T(8,128)(2,1)S(1)}, u32[]{:S(2)}, u32[]{:S(2)}) collective-permute-start(s16[160,128]{1,0:T(8,128)(2,1)S(1)} %get-tuple-element.60), channel_id=1, source_target_pairs={{0,8},{4,12},{8,0},{12,4},{16,24},{20,28},{24,16},{28,20},{1,9},{5... | collective-permute-start | bytes 122888 | tf_op jit(solution)/shard_map/middle/ppermute | solution.py:26
  31.0 2.6 %collective-permute-start.12 = (s16[160,128]{1,0:T(8,128)(2,1)S(1)}, s16[160,128]{1,0:T(8,128)(2,1)S(1)}, u32[]{:S(2)}, u32[]{:S(2)}) collective-permute-start(s16[160,128]{1,0:T(8,128)(2,1)S(1)} %get-tuple-element.67), channel_id=1, source_target_pairs={{0,16},{4,20},{8,24},{12,28},{16,0},{20,4},{24,8},{28,12},{1,17},{... | collective-permute-start | bytes 122888 | tf_op jit(solution)/shard_map/middle/ppermute | solution.py:26
  33.6 0.7 %middle.3 = (s16[160,128]{1,0:T(8,128)(2,1)S(1)}, s16[160,128]{1,0:T(8,128)(2,1)S(1)}, s16[160,128]{1,0:T(8,128)(2,1)S(1)}, s16[160,128]{1,0:T(8,128)(2,1)S(1)}) custom-call(s32[3]{0:T(128)S(1)} %pad_add_fusion.place, f32[3,192,128]{2,1,0:T(8,128)S(1)} %get-tuple-element.54.kept, s16[592,128]{1,0:T(8,128)(2,1)S(1)} %collective-permute-done.8.came), custom_call_target="tpu_custom_call" | custom-call | flops 10000000000 | bytes 610316 | tf_op jit(solution)/shard_map/middle/pallas_call | solution.py:189
  34.2 1.5 %collective-permute-start.14 = (s16[160,128]{1,0:T(8,128)(2,1)S(1)}, s16[160,128]{1,0:T(8,128)(2,1)S(1)}, u32[]{:S(2)}, u32[]{:S(2)}) collective-permute-start(s16[160,128]{1,0:T(8,128)(2,1)S(1)} %get-tuple-element.70), channel_id=1, source_target_pairs={{0,8},{4,12},{8,0},{12,4},{16,24},{20,28},{24,16},{28,20},{1,9},{5... | collective-permute-start | bytes 122888 | tf_op jit(solution)/shard_map/middle/ppermute | solution.py:26
  35.7 3.0 %collective-permute-start.15 = (s16[160,128]{1,0:T(8,128)(2,1)S(1)}, s16[160,128]{1,0:T(8,128)(2,1)S(1)}, u32[]{:S(2)}, u32[]{:S(2)}) collective-permute-start(s16[160,128]{1,0:T(8,128)(2,1)S(1)} %get-tuple-element.71), channel_id=1, source_target_pairs={{0,16},{4,20},{8,24},{12,28},{16,0},{20,4},{24,8},{28,12},{1,17},{... | collective-permute-start | bytes 122888 | tf_op jit(solution)/shard_map/middle/ppermute | solution.py:26
  38.7 3.1 %embed.1 = bf16[256,3072]{1,0:T(8,128)(2,1)} custom-call(s32[3]{0:T(128)S(1)} %pad_add_fusion.place, bf16[256,384]{1,0:T(8,128)(2,1)} %patches.5, bf16[3,256,768]{2,1,0:T(8,128)(2,1)S(1)} %embed_near.1.near, bf16[192,768]{1,0:T(8,128)(2,1)S(1)} %collective-permute-done.1.far, bf16[192,768]{1,0:T(8,128)(2,1)S(1)} %collective-permute-done.11.far_sib), custom_call_target="tpu_custom_call" | custom-call | flops 10000000000 | bytes 3538956 | tf_op jit(solution)/shard_map/embed/pallas_call | solution.py:189
  41.8 2.7 %collective-permute-done.16.refs_7_ = s16[160,128]{1,0:T(8,128)(2,1)S(1)} collective-permute-done((s16[160,128]{1,0:T(8,128)(2,1)S(1)}, s16[160,128]{1,0:T(8,128)(2,1)S(1)}, u32[]{:S(2)}, u32[]{:S(2)}) %collective-permute-start.16) | collective-permute-done | bytes 40992 | tf_op jit(solution)/shard_map/middle/ppermute | solution.py:26
  44.5 0.7 %last.1 = f32[48,768]{1,0:T(8,128)} custom-call(s16[160,128]{1,0:T(8,128)(2,1)S(1)} %get-tuple-element.74.refs_0_, s16[160,128]{1,0:T(8,128)(2,1)S(1)} %collective-permute-done.10.refs_1_, s16[160,128]{1,0:T(8,128)(2,1)S(1)} %collective-permute-done.12.refs_2_, s16[160,128]{1,0:T(8,128)(2,1)S(1)} %collective-permute-done.13.refs_3_, ...), custom_call_target="tpu_custom_call" | custom-call | tf_op jit(solution)/shard_map/last/pallas_call | solution.py:189
  (23 shorter events, 2.0 us)
Async XLA Ops:
  0.6 11.1 %collective-permute-start = (bf16[384,768]{1,0:T(8,128)(2,1)}, bf16[384,768]{1,0:T(8,128)(2,1)S(1)}, u32[]{:S(2)}, u32[]{:S(2)}) collective-permute-start(bf16[384,768]{1,0:T(8,128)(2,1)} %own.3), channel_id=1, source_target_pairs={{0,1},{1,0},{2,3},{3,2},{4,6},{5,7},{6,4},{7,5},{8,9},{9,8},{10,11... | collective-permute-start | bytes 1769480 | tf_op jit(solution)/shard_map/gather_weight/ppermute | solution.py:213
  5.6 5.7 %collective-permute-start.4 = (s32[1,2]{1,0:T(1,128)S(1)}, s32[1,2]{1,0:T(1,128)S(1)}, u32[]{:S(2)}, u32[]{:S(2)}) collective-permute-start(s32[1,2]{1,0:T(1,128)S(1)} %multiply_multiply_fusion.shares), channel_id=1, source_target_pairs={{28,0},{0,4},{4,8},{8,12},{12,16},{16,20},{20,24},{24,28},{29,1},{... | collective-permute-start | bytes 32 | tf_op jit(solution)/shard_map/shares/ppermute | solution.py:31
  9.0 5.5 %collective-permute-start.3 = (s16[4,1168,128]{2,1,0:T(8,128)(2,1)S(1)}, s16[4,1168,128]{2,1,0:T(8,128)(2,1)S(1)}, u32[]{:S(2)}, u32[]{:S(2)}) collective-permute-start(s16[4,1168,128]{2,1,0:T(8,128)(2,1)S(1)} %get-tuple-element.47), channel_id=1, source_target_pairs={{0,4},{4,0},{8,12},{12,8},{16,20},{20,16},{24,28},{28,24},{1,5},{5... | collective-permute-start | bytes 3588104 | tf_op jit(solution)/shard_map/pair/ppermute | solution.py:26
  11.3 3.2 %collective-permute-start.5 = (s32[1,2]{1,0:T(1,128)S(1)}, s32[1,2]{1,0:T(1,128)S(1)}, u32[]{:S(2)}, u32[]{:S(2)}) collective-permute-start(s32[1,2]{1,0:T(1,128)S(1)} %collective-permute-done.4.before), channel_id=1, source_target_pairs={{0,4},{4,0},{8,12},{12,8},{16,20},{20,16},{24,28},{28,24},{1,5},{5... | collective-permute-start | bytes 32 | tf_op jit(solution)/shard_map/pair/ppermute | solution.py:26
  12.3 7.4 %collective-permute-start.2 = (bf16[384,768]{1,0:T(8,128)(2,1)S(1)}, bf16[384,768]{1,0:T(8,128)(2,1)S(1)}, u32[]{:S(2)}, u32[]{:S(2)}) collective-permute-start(bf16[384,768]{1,0:T(8,128)(2,1)S(1)} %collective-permute-done.first), channel_id=1, source_target_pairs={{0,4},{4,0},{8,12},{12,8},{16,20},{20,16},{24,28},{28,24},{1,5},{5... | collective-permute-start | bytes 1769480 | tf_op jit(solution)/shard_map/relay_weight/ppermute | solution.py:26
  12.5 7.2 %collective-permute-start.1 = (bf16[192,768]{1,0:T(8,128)(2,1)S(1)}, bf16[192,768]{1,0:T(8,128)(2,1)S(1)}, u32[]{:S(2)}, u32[]{:S(2)}) collective-permute-start(bf16[192,768]{1,0:T(8,128)(2,1)S(1)} %relay_weight.1), channel_id=1, source_target_pairs={{0,2},{1,3},{2,0},{3,1},{4,5},{5,4},{6,7},{7,6},{8,10},{9,11},{10,... | collective-permute-start | bytes 884744 | tf_op jit(solution)/shard_map/relay_weight/ppermute | solution.py:213
  15.9 6.9 %collective-permute-start.6 = (s16[2,592,128]{2,1,0:T(8,128)(2,1)S(1)}, s16[2,592,128]{2,1,0:T(8,128)(2,1)S(1)}, u32[]{:S(2)}, u32[]{:S(2)}) collective-permute-start(s16[2,592,128]{2,1,0:T(8,128)(2,1)S(1)} %get-tuple-element.48), channel_id=1, source_target_pairs={{0,1},{1,0},{2,3},{3,2},{4,6},{5,7},{6,4},{7,5},{8,9},{9,8},{10,11... | collective-permute-start | bytes 909320 | tf_op jit(solution)/shard_map/pair/ppermute | solution.py:213
  17.4 8.9 %collective-permute-start.7 = (s16[2,592,128]{2,1,0:T(8,128)(2,1)S(1)}, s16[2,592,128]{2,1,0:T(8,128)(2,1)S(1)}, u32[]{:S(2)}, u32[]{:S(2)}) collective-permute-start(s16[2,592,128]{2,1,0:T(8,128)(2,1)S(1)} %get-tuple-element.52), channel_id=1, source_target_pairs={{0,1},{1,0},{2,3},{3,2},{4,6},{5,7},{6,4},{7,5},{8,9},{9,8},{10,11... | collective-permute-start | bytes 909320 | tf_op jit(solution)/shard_map/pair/ppermute | solution.py:213
  22.9 5.3 %collective-permute-start.9 = (s16[592,128]{1,0:T(8,128)(2,1)S(1)}, s16[592,128]{1,0:T(8,128)(2,1)S(1)}, u32[]{:S(2)}, u32[]{:S(2)}) collective-permute-start(s16[592,128]{1,0:T(8,128)(2,1)S(1)} %get-tuple-element.59), channel_id=1, source_target_pairs={{0,2},{1,3},{2,0},{3,1},{4,5},{5,4},{6,7},{7,6},{8,10},{9,11},{10,... | collective-permute-start | bytes 454664 | tf_op jit(solution)/shard_map/steps/ppermute | solution.py:213
  26.5 7.1 %collective-permute-start.8 = (s16[592,128]{1,0:T(8,128)(2,1)S(1)}, s16[592,128]{1,0:T(8,128)(2,1)S(1)}, u32[]{:S(2)}, u32[]{:S(2)}) collective-permute-start(s16[592,128]{1,0:T(8,128)(2,1)S(1)} %get-tuple-element.55), channel_id=1, source_target_pairs={{0,2},{1,3},{2,0},{3,1},{4,5},{5,4},{6,7},{7,6},{8,10},{9,11},{10,... | collective-permute-start | bytes 454664 | tf_op jit(solution)/shard_map/steps/ppermute | solution.py:213
  28.9 4.7 %collective-permute-start.10 = (s16[160,128]{1,0:T(8,128)(2,1)S(1)}, s16[160,128]{1,0:T(8,128)(2,1)S(1)}, u32[]{:S(2)}, u32[]{:S(2)}) collective-permute-start(s16[160,128]{1,0:T(8,128)(2,1)S(1)} %get-tuple-element.60), channel_id=1, source_target_pairs={{0,8},{4,12},{8,0},{12,4},{16,24},{20,28},{24,16},{28,20},{1,9},{5... | collective-permute-start | bytes 122888 | tf_op jit(solution)/shard_map/middle/ppermute | solution.py:26
  30.9 7.8 %collective-permute-start.11 = (bf16[192,768]{1,0:T(8,128)(2,1)S(1)}, bf16[192,768]{1,0:T(8,128)(2,1)S(1)}, u32[]{:S(2)}, u32[]{:S(2)}) collective-permute-start(bf16[192,768]{1,0:T(8,128)(2,1)S(1)} %collective-permute-done.1.far), channel_id=1, source_target_pairs={{0,4},{4,0},{8,12},{12,8},{16,20},{20,16},{24,28},{28,24},{1,5},{5... | collective-permute-start | bytes 884744 | tf_op jit(solution)/shard_map/relay_weight/ppermute | solution.py:26
  31.0 10.8 %collective-permute-start.12 = (s16[160,128]{1,0:T(8,128)(2,1)S(1)}, s16[160,128]{1,0:T(8,128)(2,1)S(1)}, u32[]{:S(2)}, u32[]{:S(2)}) collective-permute-start(s16[160,128]{1,0:T(8,128)(2,1)S(1)} %get-tuple-element.67), channel_id=1, source_target_pairs={{0,16},{4,20},{8,24},{12,28},{16,0},{20,4},{24,8},{28,12},{1,17},{... | collective-permute-start | bytes 122888 | tf_op jit(solution)/shard_map/middle/ppermute | solution.py:26
  33.5 8.2 %collective-permute-start.13 = (s16[160,128]{1,0:T(8,128)(2,1)S(1)}, s16[160,128]{1,0:T(8,128)(2,1)S(1)}, u32[]{:S(2)}, u32[]{:S(2)}) collective-permute-start(s16[160,128]{1,0:T(8,128)(2,1)S(1)} %get-tuple-element.68), channel_id=1, source_target_pairs={{0,24},{4,28},{8,16},{12,20},{16,8},{20,12},{24,0},{28,4},{1,25},{... | collective-permute-start | bytes 122888 | tf_op jit(solution)/shard_map/middle/ppermute | solution.py:26
  34.2 7.5 %collective-permute-start.14 = (s16[160,128]{1,0:T(8,128)(2,1)S(1)}, s16[160,128]{1,0:T(8,128)(2,1)S(1)}, u32[]{:S(2)}, u32[]{:S(2)}) collective-permute-start(s16[160,128]{1,0:T(8,128)(2,1)S(1)} %get-tuple-element.70), channel_id=1, source_target_pairs={{0,8},{4,12},{8,0},{12,4},{16,24},{20,28},{24,16},{28,20},{1,9},{5... | collective-permute-start | bytes 122888 | tf_op jit(solution)/shard_map/middle/ppermute | solution.py:26
  35.7 6.1 %collective-permute-start.15 = (s16[160,128]{1,0:T(8,128)(2,1)S(1)}, s16[160,128]{1,0:T(8,128)(2,1)S(1)}, u32[]{:S(2)}, u32[]{:S(2)}) collective-permute-start(s16[160,128]{1,0:T(8,128)(2,1)S(1)} %get-tuple-element.71), channel_id=1, source_target_pairs={{0,16},{4,20},{8,24},{12,28},{16,0},{20,4},{24,8},{28,12},{1,17},{... | collective-permute-start | bytes 122888 | tf_op jit(solution)/shard_map/middle/ppermute | solution.py:26
  38.7 5.8 %collective-permute-start.16 = (s16[160,128]{1,0:T(8,128)(2,1)S(1)}, s16[160,128]{1,0:T(8,128)(2,1)S(1)}, u32[]{:S(2)}, u32[]{:S(2)}) collective-permute-start(s16[160,128]{1,0:T(8,128)(2,1)S(1)} %get-tuple-element.72), channel_id=1, source_target_pairs={{0,24},{4,28},{8,16},{12,20},{16,8},{20,12},{24,0},{28,4},{1,25},{... | collective-permute-start | bytes 122888 | tf_op jit(solution)/shard_map/middle/ppermute | solution.py:26
where the time goes:
time: 45.5 us; the launch traced here: 45.2 us
  starting transfers between devices  21.2 us (47%)
  Pallas kernels  13.8 us (30%)
  waiting for transfers between devices  7.45 us (16%)
  between operations  2.04 us (4%)
  other arithmetic  0.74 us (2%)
    pallas_call x11, Pallas kernels, call(): pl.pallas_call(kernel, out_shape=outs, in_specs=[*specs] + [VMEM] * (len(...  13.8 us
    ppermute x10, starting transfers between devices, exchange(): lax.ppermute(block, axis, [(i, i ^ step) for i in range(lax.axis_size(axi...  11.2 us
    ppermute x6, starting transfers between devices, along_planes(): return lax.ppermute(block, ('dp', 'fsdp'), pairs)  9.99 us
    ppermute x6, waiting for transfers between devices, along_planes(): return lax.ppermute(block, ('dp', 'fsdp'), pairs)  4.73 us
    ppermute x10, waiting for transfers between devices, exchange(): lax.ppermute(block, axis, [(i, i ^ step) for i in range(lax.axis_size(axi...  2.71 us
  transfers between devices with their start and end apart: 17, of which 6 were waited for; matrix products, arithmetic and copies ran while one was open for 2% of the time, Pallas kernels for 22%

commit v1 on v0

--- a/solution.py
+++ b/solution.py
@@ -128,21 +128,18 @@
         still[j] = kept[0, j] + part
 
 
-def middle_kernel(depth, place, kept, came, *refs):
-    *outs, held = refs
+def middle_kernel(depth, kept, came, out, held):
     blocks, rows, _ = kept.shape
     for j, part in enumerate(get_chunk(came, rows)[0]):
         held[j] = kept[j] + part
-    for k, out in enumerate(outs):
-        here = pl.ds(pl.multiple_of((place[1] ^ k) * depth, depth), depth)
-        put_chunk(out, [held[j, here, :] for j in range(blocks)])
+    for k in range(out.shape[0]):
+        put_chunk(out.at[k], [held[j, pl.ds(k * depth, depth), :] for j in range(blocks)])
 
 
 def last_kernel(bounds, *refs):
     *ins, out = refs
-    count = len(ins) // len(bounds)
-    for i, (lo, _) in enumerate(bounds):
-        parts = [get_chunk(ref, out.shape[0])[0] for ref in ins[i * count : (i + 1) * count]]
+    for (lo, _), came in zip(bounds, ins):
+        parts = [get_chunk(came.at[k], out.shape[0])[0] for k in range(came.shape[0])]
         for j, terms in enumerate(zip(*parts)):
             out[:, lanes(lo + j)] = sum(terms[1:], terms[0])
 
@@ -152,36 +149,24 @@
     half[...] = first[pl.ds(pl.multiple_of(place[2] * rows, rows), rows), :]
 
 
-def near_kernel(place, patches, own, first, second, out, p_held, held, arrived):
+def near_kernel(place, patches, own, first, second, out):
     core = place[2]
-    copies = [
-        pltpu.make_async_copy(patches, p_held, arrived.at[0]),
-        pltpu.make_async_copy(own, held, arrived.at[1]),
-    ]
-    for copy in copies:
-        copy.start()
-    copies[0].wait()
-    out[1 + core] = times(p_held[...], first[...]).astype(BF16)
-    out[2 - core] = times(p_held[...], second[...]).astype(BF16)
-    copies[1].wait()
-    out[0] = times(p_held[...], held[...]).astype(BF16)
-
-
-def embed_kernel(place, patches, near, far, far_sib, out, p_held, halves, arrived):
+    for k, weight in ((1 + core, first), (2 - core, second), (0, own)):
+        out[k] = times(patches[...], weight[...]).astype(BF16)
+
+
+def embed_kernel(place, patches, near, far, far_sib, out, halves):
     me, core, columns = place[0], place[2], near.shape[2]
     rows = far.shape[0]
-    copy = pltpu.make_async_copy(patches, p_held, arrived)
-    copy.start()
 
     def put(k, value):
         out[:, pl.ds(pl.multiple_of((me ^ k) * columns, columns), columns)] = value
 
+    halves[0] = patches[:, :rows]
+    halves[1] = patches[:, rows:]
+    put(3, (times(halves[core], far[...]) + times(halves[1 - core], far_sib[...])).astype(BF16))
     for k in range(3):
         put(k, near[k])
-    copy.wait()
-    halves[0] = p_held[:, :rows]
-    halves[1] = p_held[:, rows:]
-    put(3, (times(halves[core], far[...]) + times(halves[1 - core], far_sib[...])).astype(BF16))
 
 
 def call(kernel, outs, operands, specs=(), scratch=(), flops=0):
@@ -271,9 +256,8 @@
         near = call(
             near_kernel,
             jax.ShapeDtypeStruct((3, tokens, columns), BF16),
-            [place, in_hbm(patches), in_hbm(weight), first, second],
-            [SMEM, HBM, HBM],
-            [pltpu.VMEM(patches.shape, BF16), pltpu.VMEM(weight.shape, BF16), pltpu.SemaphoreType.DMA((2,))],
+            [place, patches, weight, first, second],
+            [SMEM],
             flops=2 * 10**9,
         )
         near, came_parts[0] = lax.optimization_barrier((near, came_parts[0]))
@@ -295,25 +279,25 @@
     with jax.named_scope("middle"):
         sums = []
         for i, (lo, hi) in enumerate(bounds):
-            if i and 1:
-                came_parts[i], sums[1] = lax.optimization_barrier((came_parts[i], sums[1]))
-            parts = call(
+            part = call(
                 functools.partial(middle_kernel, depth),
-                [jax.ShapeDtypeStruct(chunk_shape(depth, (hi - lo) * LANES), I16)] * (count_dp // 2),
-                [place, kept_parts[i], came_parts[i]],
-                [SMEM],
+                jax.ShapeDtypeStruct((count_dp // 2, *chunk_shape(depth, (hi - lo) * LANES)), I16),
+                [kept_parts[i], came_parts[i]],
+                (),
                 [pltpu.VMEM((hi - lo, rows, LANES), F32)],
                 flops=10**10,
             )
-            sums += [exchange(part, "dp", 2 * k) if k else part for k, part in enumerate(parts)]
+            groups = [list(range(c, count_dp, 2)) for c in (0, 1)]
+            sums.append(lax.all_to_all(part, "dp", 0, 0, axis_index_groups=groups))
+            last_part = part
     with jax.named_scope("embed"):
-        near, sums[count_dp // 2] = lax.optimization_barrier((near, sums[count_dp // 2]))
+        near, _ = lax.optimization_barrier((near, last_part))
         embedded = call(
             embed_kernel,
             jax.ShapeDtypeStruct((tokens, columns * count_fsdp), BF16),
-            [place, in_hbm(patches), near, far, far_sib],
-            [SMEM, HBM],
-            [pltpu.VMEM(patches.shape, BF16), pltpu.VMEM((2, tokens, rows), BF16), pltpu.SemaphoreType.DMA],
+            [place, patches, near, far, far_sib],
+            [SMEM],
+            [pltpu.VMEM((2, tokens, rows), BF16)],
             flops=10**10,
         )
     with jax.named_scope("last"):

time: 45.5 us -> 50.7 us (1.11)
  waiting for transfers between devices: 7.45 us -> 15.9 us
  Pallas kernels: 13.8 us -> 12 us
  starting transfers between devices: 21.2 us -> 19.7 us
    all_to_all x0 -> x2, waiting for transfers between devices: none -> 9.34 us  [tiled_body(): sums.append(lax.all_to_all(part, 'dp', 0, 0, axis_index_groups=groups))]
    ppermute x10 -> x4, starting transfers between devices: 11.2 us -> 2.3 us  [exchange(): lax.ppermute(block, axis, [(i, i ^ step) for i in range(lax.axis_size(axi...]
    all_to_all x0 -> x2, starting transfers between devices: none -> 8.22 us  [tiled_body(): sums.append(lax.all_to_all(part, 'dp', 0, 0, axis_index_groups=groups))]
    ppermute x10 -> x4, waiting for transfers between devices: 2.71 us -> 0.01 us  [exchange(): lax.ppermute(block, axis, [(i, i ^ step) for i in range(lax.axis_size(axi...]
    pallas_call x11, Pallas kernels: 13.8 us -> 12 us  [call(): pl.pallas_call(kernel, out_shape=outs, in_specs=[*specs] + [VMEM] * (len(...]
    ppermute x6, waiting for transfers between devices: 4.73 us -> 6.53 us  [along_planes(): return lax.ppermute(block, ('dp', 'fsdp'), pairs)]
    ppermute x6, starting transfers between devices: 9.99 us -> 9.18 us  [along_planes(): return lax.ppermute(block, ('dp', 'fsdp'), pairs)]
  transfers between devices with their start and end apart: 17 -> 13, of which waited for: 6 -> 7; matrix products, arithmetic and copies ran while one was open for 2% -> 1% of each run, Pallas kernels for 22% -> 16%
where the time goes in v1:
time: 50.7 us; the launch traced here: 50.4 us
  starting transfers between devices  19.7 us (39%)
  waiting for transfers between devices  15.9 us (31%)
  Pallas kernels  12 us (24%)
  between operations  2.02 us (4%)
  other arithmetic  0.74 us (1%)
    pallas_call x11, Pallas kernels, call(): pl.pallas_call(kernel, out_shape=outs, in_specs=[*specs] + [VMEM] * (len(...  12 us
    all_to_all x2, waiting for transfers between devices, tiled_body(): sums.append(lax.all_to_all(part, 'dp', 0, 0, axis_index_groups=groups))  9.34 us
    ppermute x6, starting transfers between devices, along_planes(): return lax.ppermute(block, ('dp', 'fsdp'), pairs)  9.18 us
    all_to_all x2, starting transfers between devices, tiled_body(): sums.append(lax.all_to_all(part, 'dp', 0, 0, axis_index_groups=groups))  8.22 us
    ppermute x6, waiting for transfers between devices, along_planes(): return lax.ppermute(block, ('dp', 'fsdp'), pairs)  6.53 us
    ppermute x4, starting transfers between devices, exchange(): lax.ppermute(block, axis, [(i, i ^ step) for i in range(lax.axis_size(axi...  2.3 us
  transfers between devices with their start and end apart: 13, of which 7 were waited for; matrix products, arithmetic and copies ran while one was open for 1% of the time, Pallas kernels for 16%

profile of v1, /device:TPU:0, one launch (start us, length us, event | category | flops | bytes accessed | tf_op | source)
XLA Modules:
  0.0 50.4 jit_solution(2202477521395554421)
XLA Ops:
  0.6 3.0 %collective-permute-start = (bf16[384,768]{1,0:T(8,128)(2,1)}, bf16[384,768]{1,0:T(8,128)(2,1)S(1)}, u32[]{:S(2)}, u32[]{:S(2)}) collective-permute-start(bf16[384,768]{1,0:T(8,128)(2,1)} %own.3), channel_id=1, source_target_pairs={{0,1},{1,0},{2,3},{3,2},{4,6},{5,7},{6,4},{7,5},{8,9},{9,8},{10,11... | collective-permute-start | bytes 1769480 | tf_op jit(solution)/shard_map/gather_weight/ppermute | solution.py:198
  4.9 0.7 %multiply_multiply_fusion.shares = s32[1,2]{1,0:T(1,128)S(1)} fusion(s32[1,2]{1,0:T(1,128)} %param.11, s32[]{:T(128)} %bitcast.6, s32[]{:T(128)} %bitcast.5), kind=kLoop, calls=%fused_computation.1 | loop fusion | flops 4 | bytes 24 | tf_op jit(solution)/shard_map/shares/mul | solution.py:204
  5.7 3.4 %send.1 = (s16[4,1168,128]{2,1,0:T(8,128)(2,1)S(1)}, bf16[192,256]{1,0:T(8,128)(2,1)S(1)}, bf16[4,256,768]{2,1,0:T(8,128)(2,1)S(1)}) custom-call(s32[3]{0:T(128)S(1)} %pad_add_fusion.place, bf16[256,384]{1,0:T(8,128)(2,1)} %patches.5, bf16[256,3072]{1,0:T(8,128)(2,1)} %grad_embed.1, s32[1,2]{1,0:T(1,128)S(1)} %multiply_multiply_fusion.shares), custom_call_target="tpu_custom_call" | custom-call | tf_op jit(solution)/shard_map/send/pallas_call | solution.py:174
  9.0 1.8 %collective-permute-start.3 = (s16[4,1168,128]{2,1,0:T(8,128)(2,1)S(1)}, s16[4,1168,128]{2,1,0:T(8,128)(2,1)S(1)}, u32[]{:S(2)}, u32[]{:S(2)}) collective-permute-start(s16[4,1168,128]{2,1,0:T(8,128)(2,1)S(1)} %get-tuple-element.30), channel_id=1, source_target_pairs={{0,4},{4,0},{8,12},{12,8},{16,20},{20,16},{24,28},{28,24},{1,5},{5... | collective-permute-start | bytes 3588104 | tf_op jit(solution)/shard_map/pair/ppermute | solution.py:26
  11.7 0.6 %relay_weight.1 = bf16[192,768]{1,0:T(8,128)(2,1)S(1)} custom-call(s32[3]{0:T(128)S(1)} %pad_add_fusion.place, bf16[384,768]{1,0:T(8,128)(2,1)S(1)} %collective-permute-done.first), custom_call_target="tpu_custom_call" | custom-call | tf_op jit(solution)/shard_map/relay_weight/pallas_call | solution.py:174
  12.5 2.0 %collective-permute-start.1 = (bf16[192,768]{1,0:T(8,128)(2,1)S(1)}, bf16[192,768]{1,0:T(8,128)(2,1)S(1)}, u32[]{:S(2)}, u32[]{:S(2)}) collective-permute-start(bf16[192,768]{1,0:T(8,128)(2,1)S(1)} %relay_weight.1), channel_id=1, source_target_pairs={{0,2},{1,3},{2,0},{3,1},{4,5},{5,4},{6,7},{7,6},{8,10},{9,11},{10,... | collective-permute-start | bytes 884744 | tf_op jit(solution)/shard_map/relay_weight/ppermute | solution.py:198
  14.5 1.4 %pair.1 = (f32[2,3,192,128]{3,2,1,0:T(8,128)S(1)}, s16[2,592,128]{2,1,0:T(8,128)(2,1)S(1)}, f32[2,3,192,128]{3,2,1,0:T(8,128)S(1)}, s16[2,592,128]{2,1,0:T(8,128)(2,1)S(1)}) custom-call(s32[3]{0:T(128)S(1)} %pad_add_fusion.place, s32[1]{0:T(128)} %constant.34.clone.1.tokens, f32[4,6,192,128]{3,2,1,0:T(8,128)S(1)} %own.2.kept, ...), custom_call_target="tpu_custom_call" | custom-call | flops 99999997952 | bytes 5341224 | tf_op jit(solution)/shard_map/pair/pallas_call | solution.py:174
  15.9 1.6 %collective-permute-start.6 = (s16[2,592,128]{2,1,0:T(8,128)(2,1)S(1)}, s16[2,592,128]{2,1,0:T(8,128)(2,1)S(1)}, u32[]{:S(2)}, u32[]{:S(2)}) collective-permute-start(s16[2,592,128]{2,1,0:T(8,128)(2,1)S(1)} %get-tuple-element.31), channel_id=1, source_target_pairs={{0,1},{1,0},{2,3},{3,2},{4,6},{5,7},{6,4},{7,5},{8,9},{9,8},{10,11... | collective-permute-start | bytes 909320 | tf_op jit(solution)/shard_map/pair/ppermute | solution.py:198
  17.5 0.5 %collective-permute-start.7 = (s16[2,592,128]{2,1,0:T(8,128)(2,1)S(1)}, s16[2,592,128]{2,1,0:T(8,128)(2,1)S(1)}, u32[]{:S(2)}, u32[]{:S(2)}) collective-permute-start(s16[2,592,128]{2,1,0:T(8,128)(2,1)S(1)} %get-tuple-element.35), channel_id=1, source_target_pairs={{0,1},{1,0},{2,3},{3,2},{4,6},{5,7},{6,4},{7,5},{8,9},{9,8},{10,11... | collective-permute-start | bytes 909320 | tf_op jit(solution)/shard_map/pair/ppermute | solution.py:198
  18.0 1.7 %collective-permute-done.1.far = bf16[192,768]{1,0:T(8,128)(2,1)S(1)} collective-permute-done((bf16[192,768]{1,0:T(8,128)(2,1)S(1)}, bf16[192,768]{1,0:T(8,128)(2,1)S(1)}, u32[]{:S(2)}, u32[]{:S(2)}) %collective-permute-start.1) | collective-permute-done | bytes 294944 | tf_op jit(solution)/shard_map/relay_weight/ppermute | solution.py:198
  19.7 1.3 %embed_near.1.near = bf16[3,256,768]{2,1,0:T(8,128)(2,1)S(1)} custom-call(s32[3]{0:T(128)S(1)} %pad_add_fusion.place, bf16[256,384]{1,0:T(8,128)(2,1)S(1)} %copy-done, bf16[384,768]{1,0:T(8,128)(2,1)S(1)} %copy-done.1, bf16[384,768]{1,0:T(8,128)(2,1)S(1)} %collective-permute-done.first, bf16[384,768]{1,0:T(8,128)(2,1)S(1)} %collective-permute-done.2.second), custom_call_target="tpu_custom_call" | custom-call | flops 2000000000 | bytes 3145740 | tf_op jit(solution)/shard_map/embed_near/pallas_call | solution.py:174
  21.1 1.7 %collective-permute-done.6.came = s16[2,592,128]{2,1,0:T(8,128)(2,1)S(1)} collective-permute-done((s16[2,592,128]{2,1,0:T(8,128)(2,1)S(1)}, s16[2,592,128]{2,1,0:T(8,128)(2,1)S(1)}, u32[]{:S(2)}, u32[]{:S(2)}) %collective-permute-start.6) | collective-permute-done | bytes 303136 | tf_op jit(solution)/shard_map/pair/ppermute | solution.py:198
  22.9 1.2 %collective-permute-start.10 = (s16[592,128]{1,0:T(8,128)(2,1)S(1)}, s16[592,128]{1,0:T(8,128)(2,1)S(1)}, u32[]{:S(2)}, u32[]{:S(2)}) collective-permute-start(s16[592,128]{1,0:T(8,128)(2,1)S(1)} %get-tuple-element.44), channel_id=1, source_target_pairs={{0,2},{1,3},{2,0},{3,1},{4,5},{5,4},{6,7},{7,6},{8,10},{9,11},{10,... | collective-permute-start | bytes 454664 | tf_op jit(solution)/shard_map/steps/ppermute | solution.py:198
  24.2 2.2 %collective-permute-done.7.came = s16[2,592,128]{2,1,0:T(8,128)(2,1)S(1)} collective-permute-done((s16[2,592,128]{2,1,0:T(8,128)(2,1)S(1)}, s16[2,592,128]{2,1,0:T(8,128)(2,1)S(1)}, u32[]{:S(2)}, u32[]{:S(2)}) %collective-permute-start.7) | collective-permute-done | bytes 303136 | tf_op jit(solution)/shard_map/pair/ppermute | solution.py:198
  26.5 0.9 %collective-permute-start.8 = (s16[592,128]{1,0:T(8,128)(2,1)S(1)}, s16[592,128]{1,0:T(8,128)(2,1)S(1)}, u32[]{:S(2)}, u32[]{:S(2)}) collective-permute-start(s16[592,128]{1,0:T(8,128)(2,1)S(1)} %get-tuple-element.38), channel_id=1, source_target_pairs={{0,2},{1,3},{2,0},{3,1},{4,5},{5,4},{6,7},{7,6},{8,10},{9,11},{10,... | collective-permute-start | bytes 454664 | tf_op jit(solution)/shard_map/steps/ppermute | solution.py:198
  27.7 0.5 %collective-permute-done.10.came = s16[592,128]{1,0:T(8,128)(2,1)S(1)} collective-permute-done((s16[592,128]{1,0:T(8,128)(2,1)S(1)}, s16[592,128]{1,0:T(8,128)(2,1)S(1)}, u32[]{:S(2)}, u32[]{:S(2)}) %collective-permute-start.10) | collective-permute-done | bytes 151584 | tf_op jit(solution)/shard_map/steps/ppermute | solution.py:198
  28.2 0.8 %middle.3 = s16[4,160,128]{2,1,0:T(8,128)(2,1)} custom-call(f32[3,192,128]{2,1,0:T(8,128)S(1)} %get-tuple-element.43.kept, s16[592,128]{1,0:T(8,128)(2,1)S(1)} %collective-permute-done.10.came), custom_call_target="tpu_custom_call" | custom-call | flops 10000000000 | bytes 610304 | tf_op jit(solution)/shard_map/middle/pallas_call | solution.py:174
  29.0 4.9 %all-to-all-start = ((s16[4,160,128]{2,1,0:T(8,128)(2,1)}), s16[4,160,128]{2,1,0:T(8,128)(2,1)S(1)}, u32[]{:S(2)}, u32[]{:S(2)}) async-start(s16[4,160,128]{2,1,0:T(8,128)(2,1)} %middle.3), calls=%async_computation | async-start | bytes 327680 | tf_op jit(solution)/shard_map/middle/all_to_all | solution.py:291
  33.9 0.8 %middle.2 = s16[4,160,128]{2,1,0:T(8,128)(2,1)} custom-call(f32[3,192,128]{2,1,0:T(8,128)S(1)} %get-tuple-element.37.kept, s16[592,128]{1,0:T(8,128)(2,1)S(1)} %collective-permute-done.8.came), custom_call_target="tpu_custom_call" | custom-call | flops 10000000000 | bytes 610304 | tf_op jit(solution)/shard_map/middle/pallas_call | solution.py:174
  34.7 5.6 %all-to-all-done.refs_0_ = s16[4,160,128]{2,1,0:T(8,128)(2,1)S(1)} async-done(((s16[4,160,128]{2,1,0:T(8,128)(2,1)}), s16[4,160,128]{2,1,0:T(8,128)(2,1)S(1)}, u32[]{:S(2)}, u32[]{:S(2)}) %all-to-all-start) | async-done | bytes 163872 | tf_op jit(solution)/shard_map/middle/all_to_all | solution.py:291
  40.3 3.3 %all-to-all-start.1 = ((s16[4,160,128]{2,1,0:T(8,128)(2,1)}), s16[4,160,128]{2,1,0:T(8,128)(2,1)S(1)}, u32[]{:S(2)}, u32[]{:S(2)}) async-start(s16[4,160,128]{2,1,0:T(8,128)(2,1)} %middle.2), calls=%async_computation.1 | async-start | bytes 327680 | tf_op jit(solution)/shard_map/middle/all_to_all | solution.py:291
  43.7 2.3 %embed.1 = bf16[256,3072]{1,0:T(8,128)(2,1)} custom-call(s32[3]{0:T(128)S(1)} %pad_add_fusion.place, bf16[256,384]{1,0:T(8,128)(2,1)S(1)} %copy-done, bf16[3,256,768]{2,1,0:T(8,128)(2,1)S(1)} %embed_near.1.near, bf16[192,768]{1,0:T(8,128)(2,1)S(1)} %collective-permute-done.1.far, bf16[192,768]{1,0:T(8,128)(2,1)S(1)} %collective-permute-done.9.far_sib), custom_call_target="tpu_custom_call" | custom-call | flops 10000000000 | bytes 3538956 | tf_op jit(solution)/shard_map/embed/pallas_call | solution.py:174
  45.9 3.7 %all-to-all-done.1.refs_1_ = s16[4,160,128]{2,1,0:T(8,128)(2,1)S(1)} async-done(((s16[4,160,128]{2,1,0:T(8,128)(2,1)}), s16[4,160,128]{2,1,0:T(8,128)(2,1)S(1)}, u32[]{:S(2)}, u32[]{:S(2)}) %all-to-all-start.1) | async-done | bytes 163872 | tf_op jit(solution)/shard_map/middle/all_to_all | solution.py:291
  49.6 0.7 %last.1 = f32[48,768]{1,0:T(8,128)} custom-call(s16[4,160,128]{2,1,0:T(8,128)(2,1)S(1)} %all-to-all-done.refs_0_, s16[4,160,128]{2,1,0:T(8,128)(2,1)S(1)} %all-to-all-done.1.refs_1_), custom_call_target="tpu_custom_call" | custom-call | tf_op jit(solution)/shard_map/last/pallas_call | solution.py:174
  (19 shorter events, 1.8 us)
Async XLA Ops:
  0.6 11.1 %collective-permute-start = (bf16[384,768]{1,0:T(8,128)(2,1)}, bf16[384,768]{1,0:T(8,128)(2,1)S(1)}, u32[]{:S(2)}, u32[]{:S(2)}) collective-permute-start(bf16[384,768]{1,0:T(8,128)(2,1)} %own.3), channel_id=1, source_target_pairs={{0,1},{1,0},{2,3},{3,2},{4,6},{5,7},{6,4},{7,5},{8,9},{9,8},{10,11... | collective-permute-start | bytes 1769480 | tf_op jit(solution)/shard_map/gather_weight/ppermute | solution.py:198
  5.6 5.7 %collective-permute-start.4 = (s32[1,2]{1,0:T(1,128)S(1)}, s32[1,2]{1,0:T(1,128)S(1)}, u32[]{:S(2)}, u32[]{:S(2)}) collective-permute-start(s32[1,2]{1,0:T(1,128)S(1)} %multiply_multiply_fusion.shares), channel_id=1, source_target_pairs={{28,0},{0,4},{4,8},{8,12},{12,16},{16,20},{20,24},{24,28},{29,1},{... | collective-permute-start | bytes 32 | tf_op jit(solution)/shard_map/shares/ppermute | solution.py:31
  9.0 5.5 %collective-permute-start.3 = (s16[4,1168,128]{2,1,0:T(8,128)(2,1)S(1)}, s16[4,1168,128]{2,1,0:T(8,128)(2,1)S(1)}, u32[]{:S(2)}, u32[]{:S(2)}) collective-permute-start(s16[4,1168,128]{2,1,0:T(8,128)(2,1)S(1)} %get-tuple-element.30), channel_id=1, source_target_pairs={{0,4},{4,0},{8,12},{12,8},{16,20},{20,16},{24,28},{28,24},{1,5},{5... | collective-permute-start | bytes 3588104 | tf_op jit(solution)/shard_map/pair/ppermute | solution.py:26
  11.3 3.2 %collective-permute-start.5 = (s32[1,2]{1,0:T(1,128)S(1)}, s32[1,2]{1,0:T(1,128)S(1)}, u32[]{:S(2)}, u32[]{:S(2)}) collective-permute-start(s32[1,2]{1,0:T(1,128)S(1)} %collective-permute-done.4.before), channel_id=1, source_target_pairs={{0,4},{4,0},{8,12},{12,8},{16,20},{20,16},{24,28},{28,24},{1,5},{5... | collective-permute-start | bytes 32 | tf_op jit(solution)/shard_map/pair/ppermute | solution.py:26
  12.3 7.4 %copy-start = (bf16[256,384]{1,0:T(8,128)(2,1)S(1)}, bf16[256,384]{1,0:T(8,128)(2,1)}, u32[]{:S(2)}) copy-start(bf16[256,384]{1,0:T(8,128)(2,1)} %patches.5) | copy-start | bytes 589828
  12.3 7.4 %copy-start.1 = (bf16[384,768]{1,0:T(8,128)(2,1)S(1)}, bf16[384,768]{1,0:T(8,128)(2,1)}, u32[]{:S(2)}) copy-start(bf16[384,768]{1,0:T(8,128)(2,1)} %own.3) | copy-start | bytes 1769476
  12.3 7.4 %collective-permute-start.2 = (bf16[384,768]{1,0:T(8,128)(2,1)S(1)}, bf16[384,768]{1,0:T(8,128)(2,1)S(1)}, u32[]{:S(2)}, u32[]{:S(2)}) collective-permute-start(bf16[384,768]{1,0:T(8,128)(2,1)S(1)} %collective-permute-done.first), channel_id=1, source_target_pairs={{0,4},{4,0},{8,12},{12,8},{16,20},{20,16},{24,28},{28,24},{1,5},{5... | collective-permute-start | bytes 1769480 | tf_op jit(solution)/shard_map/relay_weight/ppermute | solution.py:26
  12.5 7.2 %collective-permute-start.1 = (bf16[192,768]{1,0:T(8,128)(2,1)S(1)}, bf16[192,768]{1,0:T(8,128)(2,1)S(1)}, u32[]{:S(2)}, u32[]{:S(2)}) collective-permute-start(bf16[192,768]{1,0:T(8,128)(2,1)S(1)} %relay_weight.1), channel_id=1, source_target_pairs={{0,2},{1,3},{2,0},{3,1},{4,5},{5,4},{6,7},{7,6},{8,10},{9,11},{10,... | collective-permute-start | bytes 884744 | tf_op jit(solution)/shard_map/relay_weight/ppermute | solution.py:198
  15.9 6.9 %collective-permute-start.6 = (s16[2,592,128]{2,1,0:T(8,128)(2,1)S(1)}, s16[2,592,128]{2,1,0:T(8,128)(2,1)S(1)}, u32[]{:S(2)}, u32[]{:S(2)}) collective-permute-start(s16[2,592,128]{2,1,0:T(8,128)(2,1)S(1)} %get-tuple-element.31), channel_id=1, source_target_pairs={{0,1},{1,0},{2,3},{3,2},{4,6},{5,7},{6,4},{7,5},{8,9},{9,8},{10,11... | collective-permute-start | bytes 909320 | tf_op jit(solution)/shard_map/pair/ppermute | solution.py:198
  17.5 8.9 %collective-permute-start.7 = (s16[2,592,128]{2,1,0:T(8,128)(2,1)S(1)}, s16[2,592,128]{2,1,0:T(8,128)(2,1)S(1)}, u32[]{:S(2)}, u32[]{:S(2)}) collective-permute-start(s16[2,592,128]{2,1,0:T(8,128)(2,1)S(1)} %get-tuple-element.35), channel_id=1, source_target_pairs={{0,1},{1,0},{2,3},{3,2},{4,6},{5,7},{6,4},{7,5},{8,9},{9,8},{10,11... | collective-permute-start | bytes 909320 | tf_op jit(solution)/shard_map/pair/ppermute | solution.py:198
  22.9 5.3 %collective-permute-start.10 = (s16[592,128]{1,0:T(8,128)(2,1)S(1)}, s16[592,128]{1,0:T(8,128)(2,1)S(1)}, u32[]{:S(2)}, u32[]{:S(2)}) collective-permute-start(s16[592,128]{1,0:T(8,128)(2,1)S(1)} %get-tuple-element.44), channel_id=1, source_target_pairs={{0,2},{1,3},{2,0},{3,1},{4,5},{5,4},{6,7},{7,6},{8,10},{9,11},{10,... | collective-permute-start | bytes 454664 | tf_op jit(solution)/shard_map/steps/ppermute | solution.py:198
  26.5 7.3 %collective-permute-start.8 = (s16[592,128]{1,0:T(8,128)(2,1)S(1)}, s16[592,128]{1,0:T(8,128)(2,1)S(1)}, u32[]{:S(2)}, u32[]{:S(2)}) collective-permute-start(s16[592,128]{1,0:T(8,128)(2,1)S(1)} %get-tuple-element.38), channel_id=1, source_target_pairs={{0,2},{1,3},{2,0},{3,1},{4,5},{5,4},{6,7},{7,6},{8,10},{9,11},{10,... | collective-permute-start | bytes 454664 | tf_op jit(solution)/shard_map/steps/ppermute | solution.py:198
  27.4 16.2 %collective-permute-start.9 = (bf16[192,768]{1,0:T(8,128)(2,1)S(1)}, bf16[192,768]{1,0:T(8,128)(2,1)S(1)}, u32[]{:S(2)}, u32[]{:S(2)}) collective-permute-start(bf16[192,768]{1,0:T(8,128)(2,1)S(1)} %collective-permute-done.1.far), channel_id=1, source_target_pairs={{0,4},{4,0},{8,12},{12,8},{16,20},{20,16},{24,28},{28,24},{1,5},{5... | collective-permute-start | bytes 884744 | tf_op jit(solution)/shard_map/relay_weight/ppermute | solution.py:26
  29.0 11.3 %all-to-all-start = ((s16[4,160,128]{2,1,0:T(8,128)(2,1)}), s16[4,160,128]{2,1,0:T(8,128)(2,1)S(1)}, u32[]{:S(2)}, u32[]{:S(2)}) async-start(s16[4,160,128]{2,1,0:T(8,128)(2,1)} %middle.3), calls=%async_computation | async-start | bytes 327680 | tf_op jit(solution)/shard_map/middle/all_to_all | solution.py:291
  40.3 9.3 %all-to-all-start.1 = ((s16[4,160,128]{2,1,0:T(8,128)(2,1)}), s16[4,160,128]{2,1,0:T(8,128)(2,1)S(1)}, u32[]{:S(2)}, u32[]{:S(2)}) async-start(s16[4,160,128]{2,1,0:T(8,128)(2,1)} %middle.2), calls=%async_computation.1 | async-start | bytes 327680 | tf_op jit(solution)/shard_map/middle/all_to_all | solution.py:291
